TPU v7x, 32 devices: a whole 2x2x4 slice. The times are simulated.
32 devices in a mesh: groups: 2 (over y), section: 4 (over z), fsdp: 4 (over x, core).
Axes of the slice: x: 2, y: 2, z: 4, core: 2. Of those that a mesh axis runs over, the one named last changes fastest.
Arguments:
- sent_act: bfloat16 [4, 1024, 4096], P('section', 'groups', 'fsdp'), parts along dimension 1, may hold values from -6 to 6
- sent_grad: bfloat16 [4, 1024, 4096], P('section', 'groups', 'fsdp'), parts along dimension 1, may hold values from -6 to 6
- stash_in: bfloat16 [4, 2, 1024, 4096], P('section', None, 'groups', 'fsdp'), parts along dimension 2, may hold values from -6 to 6
- stash_pre: bfloat16 [4, 2, 1024, 4096], P('section', None, 'groups', 'fsdp'), parts along dimension 2, may hold values from -6 to 6
- layer_weight: bfloat16 [4, 4096, 4096], P('section', None, 'fsdp'), may hold values from -0.125 to 0.125
- layer_bias: float32 [4, 4096], P('section', 'fsdp'), may hold values from -3 to 3
- seg_table: bfloat16 [4784, 4096], P('section', 'fsdp'), may hold values from -6 to 6
- seg_index: int32 [1024, 32], P('groups'), parts along dimension 0, may hold values from 0 to 4783
- seg_amp: float32 [1024, 32], P('groups'), parts along dimension 0, may hold values from -1.2 to 1.2
- field_angle: float32 [1024, 2], P('groups'), parts along dimension 0, may hold values from -1 to 1
- angle_weight: float32 [2, 4096], P(None, 'fsdp'), may hold values from -3 to 3
- target: bfloat16 [1024, 4096], P('groups', 'fsdp'), parts along dimension 0, may hold values from -6 to 6
- sched: int32 [4], P('section'), may hold values from 0 to 1
Outputs:
- fwd_out: bfloat16 [4, 1024, 4096], P('section', 'groups', 'fsdp'), parts along dimension 1
- grad_in: bfloat16 [4, 1024, 4096], P('section', 'groups', 'fsdp'), parts along dimension 1
- grad_w: bfloat16 [4, 8192, 4096], P('section', 'groups', 'fsdp'), parts along dimension 1
- grad_bias: float32 [4, 8192], P('section', ('groups', 'fsdp')), parts along dimension 1
There are 2 independent parts, one for each index of `groups`. A program takes and returns all parts, laid end to end along the dimension named above; an argument that names none is the same for every part. Nothing has to cross between parts.
All inputs are finite; a program needn't handle non-finite values.
Results may differ from a plain program's by a relative error of at most 0.017.
Values may be sent and summed in bfloat16 or wider, within the bound.
A program may use at most 128 MiB of HBM per device.

v0:
```python
import jax
import jax.numpy as jnp
from jax import lax
from jax.sharding import PartitionSpec as P


def from_behind(shard, axis, by):
    length = lax.axis_size(axis)
    pairs = [(i, i + by) for i in range(length) if 0 <= i + by < length]
    return lax.ppermute(shard, axis, pairs)


def lookup_sum(full_table, seg_index, seg_amp, first_row):
    row_count = full_table.shape[0]
    feature_count = full_table.shape[1]
    block_rows = 512
    block_count = (row_count + block_rows - 1) // block_rows
    padded = jnp.pad(full_table, ((0, block_count * block_rows - row_count), (0, 0)))
    blocks = padded.reshape(block_count, block_rows, feature_count)
    starts = jnp.arange(block_count, dtype=jnp.int32) * block_rows
    local_row = seg_index - first_row

    def add_block(total, item):
        table_block, start = item
        position = start + jnp.arange(block_rows, dtype=jnp.int32)
        matched = local_row[:, :, None] == position[None, None, :]
        amplitude = jnp.sum(jnp.where(matched, seg_amp[:, :, None], 0.0), axis=1)
        upper = amplitude.astype(jnp.bfloat16)
        lower = (amplitude - upper.astype(jnp.float32)).astype(jnp.bfloat16)
        total = total + jnp.dot(upper, table_block, preferred_element_type=jnp.float32)
        total = total + jnp.dot(lower, table_block, preferred_element_type=jnp.float32)
        return (total, None)

    empty = jnp.zeros((seg_index.shape[0], feature_count), jnp.float32)
    summed, unused = lax.scan(add_block, empty, (blocks, starts))
    return summed


def local(
    sent_act,
    sent_grad,
    stash_in,
    stash_pre,
    layer_weight,
    layer_bias,
    seg_table,
    seg_index,
    seg_amp,
    field_angle,
    angle_weight,
    target,
    sched,
):
    section_index = lax.axis_index("section")
    section_count = lax.axis_size("section")
    partial_value = lookup_sum(seg_table, seg_index, seg_amp, section_index * seg_table.shape[0])
    embedded = lax.psum(partial_value.astype(jnp.bfloat16), "section").astype(jnp.float32)
    angular = jnp.dot(field_angle, angle_weight, precision=lax.Precision.HIGHEST)
    first_input = (embedded + angular).astype(jnp.bfloat16)
    arrived = from_behind(sent_act[0], "section", 1)
    layer_input = jnp.where(section_index == 0, first_input, arrived)
    from_next = from_behind(sent_grad[0], "section", -1)
    stash_slot = sched[0]
    stashed_in = lax.dynamic_index_in_dim(stash_in[0], stash_slot, 0, keepdims=False)
    stashed_pre = lax.dynamic_index_in_dim(stash_pre[0], stash_slot, 0, keepdims=False)
    stashed_act, pullback = jax.vjp(jax.nn.gelu, stashed_pre.astype(jnp.float32))
    cotangent = jnp.where(
        section_index == section_count - 1,
        stashed_act - target.astype(jnp.float32),
        from_next.astype(jnp.float32),
    )
    pre_grad = pullback(cotangent)[0].astype(jnp.bfloat16)
    grad_bias = jnp.sum(pre_grad.astype(jnp.float32), axis=0)
    weight = layer_weight[0]
    pre_total = jnp.dot(
        lax.all_gather(layer_input, "fsdp", axis=1, tiled=True),
        weight,
        preferred_element_type=jnp.float32,
    )
    grad_total = lax.dot_general(
        lax.all_gather(stashed_in, "fsdp", axis=1, tiled=True),
        pre_grad,
        (((0,), (0,)), ((), ())),
        preferred_element_type=jnp.float32,
    )
    fwd_out = jax.nn.gelu(pre_total + layer_bias[0]).astype(jnp.bfloat16)
    partial_terms = lax.dot_general(
        pre_grad, weight, (((1,), (1,)), ((), ())), preferred_element_type=jnp.float32
    )
    grad_in = lax.psum_scatter(
        partial_terms.astype(jnp.bfloat16), "fsdp", scatter_dimension=1, tiled=True
    )
    return (fwd_out[None], grad_in[None], grad_total.astype(jnp.bfloat16)[None], grad_bias[None])


def solution(mesh):
    return jax.shard_map(
        local,
        mesh=mesh,
        in_specs=(
            P("section", "groups", "fsdp"),
            P("section", "groups", "fsdp"),
            P("section", None, "groups", "fsdp"),
            P("section", None, "groups", "fsdp"),
            P("section", None, "fsdp"),
            P("section", "fsdp"),
            P("section", "fsdp"),
            P("groups", None),
            P("groups", None),
            P("groups", None),
            P(None, "fsdp"),
            P("groups", "fsdp"),
            P("section"),
        ),
        out_specs=(
            P("section", "groups", "fsdp"),
            P("section", "groups", "fsdp"),
            P("section", "groups", "fsdp"),
            P("section", ("groups", "fsdp")),
        ),
        check_vma=False,
    )
```

profile of v0, /device:TPU:0, one launch (start us, length us, event | category | flops | bytes accessed | tf_op | source)
XLA Modules:
  0.0 238.5 jit_solution(12005963658422066757)
XLA Ops:
  10.9 3.7 %pad.4 = bf16[1536,1024]{1,0:T(8,128)(2,1)} pad(bf16[1196,1024]{1,0:T(8,128)(2,1)} %param.21, bf16[]{:T(256)} %constant.37.clone.1), padding=0_340x0_0 | pad | bytes 5595138 | tf_op jit(solution)/shard_map/jit(_pad)/pad | solution.py:18
  14.6 53.6 %while.11 = (s32[]{:T(128)}, f32[512,1024]{1,0:T(8,128)}, s32[512,32]{1,0:T(8,128)}, s32[3]{0:T(128)S(1)}, f32[512,32]{1,0:T(8,128)S(1)}, /*index=5*/bf16[3,512,1024]{2,1,0:T(8,128)(2,1)}, s32[]{:T(128)}, s32[]{:T(128)}) while((s32[]{:T(128)}, f32[512,1024]{1,0:T(8,128)}, s32[512,32]{1,0:T(8,128)}, s32[3]{0:T(128)S(1)}, ...), condition=%wide.region_2.3_spmd.clone, body=%wide.region_0.2_spmd.clone.sunk | while | flops 1101529600 | bytes 13766783 | solution.py:35
  15.8 9.0 %select_reduce_fusion.2 = f32[512,512]{1,0:T(8,128)S(1)} fusion(f32[512,32]{1,0:T(8,128)S(1)} %get-tuple-element.135, s32[512]{0:T(512)S(1)} %iota_add_fusion.2, s32[512,32]{1,0:T(8,128)} %get-tuple-element.133), kind=kLoop, calls=%fused_computation.clone.1 | loop fusion | flops 24903680 | bytes 1181696 | tf_op jit(solution)/shard_map/while/body/eval_jaxpr/reduce_sum | solution.py:27
  24.8 3.3 %fusion.57 = f32[512,1024]{1,0:T(8,128)} fusion(bf16[3,512,1024]{2,1,0:T(8,128)(2,1)} %get-tuple-element.136, s32[]{:T(128)S(6)} %copy.23, f32[512,512]{1,0:T(8,128)S(1)} %select_reduce_fusion.2), kind=kOutput, calls=%fused_computation.4.clone.1 | convolution fusion | flops 537133056 | bytes 4194308 | tf_op jit(solution)/shard_map/while/body/eval_jaxpr/dot_general | solution.py:30
  28.1 4.0 %fusion.58 = f32[512,1024]{1,0:T(8,128)} fusion(f32[512,1024]{1,0:T(8,128)} %fusion.57, f32[512,1024]{1,0:T(8,128)} %get-tuple-element.124, pred[]{:T(512)S(6)} %compare.4, bf16[3,512,1024]{2,1,0:T(8,128)(2,1)} %get-tuple-element.136, s32[]{:T(128)S(6)} %copy.23, f32[512,512]{1,0:T(8,128)S(1)} %select_reduce_fusion.2), kind=kOutput, calls=%fused_computation.2.clone.1 | convolution fusion | flops 539492352 | bytes 8388613 | tf_op jit(solution)/shard_map/while/body/eval_jaxpr/dot_general | solution.py:31
  33.3 9.0 %select_reduce_fusion.2 = f32[512,512]{1,0:T(8,128)S(1)} fusion(f32[512,32]{1,0:T(8,128)S(1)} %get-tuple-element.135, s32[512]{0:T(512)S(1)} %iota_add_fusion.2, s32[512,32]{1,0:T(8,128)} %get-tuple-element.133), kind=kLoop, calls=%fused_computation.clone.1 | loop fusion | flops 24903680 | bytes 1181696 | tf_op jit(solution)/shard_map/while/body/eval_jaxpr/reduce_sum | solution.py:27
  42.3 3.3 %fusion.57 = f32[512,1024]{1,0:T(8,128)} fusion(bf16[3,512,1024]{2,1,0:T(8,128)(2,1)} %get-tuple-element.136, s32[]{:T(128)S(6)} %copy.23, f32[512,512]{1,0:T(8,128)S(1)} %select_reduce_fusion.2), kind=kOutput, calls=%fused_computation.4.clone.1 | convolution fusion | flops 537133056 | bytes 4194308 | tf_op jit(solution)/shard_map/while/body/eval_jaxpr/dot_general | solution.py:30
  45.6 4.6 %fusion.58 = f32[512,1024]{1,0:T(8,128)} fusion(f32[512,1024]{1,0:T(8,128)} %fusion.57, f32[512,1024]{1,0:T(8,128)} %get-tuple-element.124, pred[]{:T(512)S(6)} %compare.4, bf16[3,512,1024]{2,1,0:T(8,128)(2,1)} %get-tuple-element.136, s32[]{:T(128)S(6)} %copy.23, f32[512,512]{1,0:T(8,128)S(1)} %select_reduce_fusion.2), kind=kOutput, calls=%fused_computation.2.clone.1 | convolution fusion | flops 539492352 | bytes 8388613 | tf_op jit(solution)/shard_map/while/body/eval_jaxpr/dot_general | solution.py:31
  51.4 9.0 %select_reduce_fusion.2 = f32[512,512]{1,0:T(8,128)S(1)} fusion(f32[512,32]{1,0:T(8,128)S(1)} %get-tuple-element.135, s32[512]{0:T(512)S(1)} %iota_add_fusion.2, s32[512,32]{1,0:T(8,128)} %get-tuple-element.133), kind=kLoop, calls=%fused_computation.clone.1 | loop fusion | flops 24903680 | bytes 1181696 | tf_op jit(solution)/shard_map/while/body/eval_jaxpr/reduce_sum | solution.py:27
  60.4 3.3 %fusion.57 = f32[512,1024]{1,0:T(8,128)} fusion(bf16[3,512,1024]{2,1,0:T(8,128)(2,1)} %get-tuple-element.136, s32[]{:T(128)S(6)} %copy.23, f32[512,512]{1,0:T(8,128)S(1)} %select_reduce_fusion.2), kind=kOutput, calls=%fused_computation.4.clone.1 | convolution fusion | flops 537133056 | bytes 4194308 | tf_op jit(solution)/shard_map/while/body/eval_jaxpr/dot_general | solution.py:30
  63.6 4.6 %fusion.58 = f32[512,1024]{1,0:T(8,128)} fusion(f32[512,1024]{1,0:T(8,128)} %fusion.57, f32[512,1024]{1,0:T(8,128)} %get-tuple-element.124, pred[]{:T(512)S(6)} %compare.4, bf16[3,512,1024]{2,1,0:T(8,128)(2,1)} %get-tuple-element.136, s32[]{:T(128)S(6)} %copy.23, f32[512,512]{1,0:T(8,128)S(1)} %select_reduce_fusion.2), kind=kOutput, calls=%fused_computation.2.clone.1 | convolution fusion | flops 539492352 | bytes 8388613 | tf_op jit(solution)/shard_map/while/body/eval_jaxpr/dot_general | solution.py:31
  68.2 2.7 %convert_element_type.47 = bf16[512,1024]{1,0:T(8,128)(2,1)} convert(f32[512,1024]{1,0:T(8,128)} %get-tuple-element.36) | non-fusion elementwise | flops 524288 | bytes 3145728 | tf_op jit(solution)/shard_map/convert_element_type | solution.py:57
  72.9 5.9 %collective-permute-start = (bf16[512,1024]{1,0:T(8,128)(2,1)}, bf16[512,1024]{1,0:T(8,128)(2,1)}, u32[]{:S(2)}, u32[]{:S(2)}) collective-permute-start(bf16[512,1024]{1,0:T(8,128)(2,1)} %bitcast.1), channel_id=1, source_target_pairs={{0,4},{4,8},{8,12},{1,5},{5,9},{9,13},{2,6},{6,10},{10,14},{3,7},{... | collective-permute-start | bytes 3145736 | tf_op jit(solution)/shard_map/ppermute | solution.py:10
  78.8 38.6 %collective-permute-done = bf16[512,1024]{1,0:T(8,128)(2,1)} collective-permute-done((bf16[512,1024]{1,0:T(8,128)(2,1)}, bf16[512,1024]{1,0:T(8,128)(2,1)}, u32[]{:S(2)}, u32[]{:S(2)}) %collective-permute-start) | collective-permute-done | bytes 1048608 | tf_op jit(solution)/shard_map/ppermute | solution.py:10
  117.4 23.2 %all-reduce.3.cloned.1.call-done = bf16[512,1024]{1,0:T(8,128)(2,1)} async-done(((bf16[512,1024]{1,0:T(8,128)(2,1)}), bf16[512,1024]{1,0:T(8,128)(2,1)}) %all-reduce.3.cloned.1.call-update) | async-done | bytes 1048592 | tf_op jit(solution)/shard_map/psum | solution.py:57
  140.7 4.2 %fusion.42 = bf16[512,1024]{1,0:T(8,128)(2,1)} fusion(bf16[512,1024]{1,0:T(8,128)(2,1)} %collective-permute-done, f32[512,2]{0,1:T(2,128)S(1)} %copy-done.5, f32[2,1024]{1,0:T(2,128)S(1)} %copy-done.4, bf16[512,1024]{1,0:T(8,128)(2,1)} %all-reduce.3.cloned.1.call-done, pred[]{:T(512)S(6)} %eq.19), kind=kOutput, calls=%fused_computation.49 | convolution fusion | flops 14680064 | bytes 3158017 | tf_op jit(solution)/shard_map/dot_general | solution.py:58
  144.9 1.5 collective-permute-start.1
  146.4 25.8 %collective-permute-done.1 = bf16[512,1024]{1,0:T(8,128)(2,1)} collective-permute-done((bf16[512,1024]{1,0:T(8,128)(2,1)}, bf16[512,1024]{1,0:T(8,128)(2,1)}, u32[]{:S(2)}, u32[]{:S(2)}) %collective-permute-start.1) | collective-permute-done | bytes 1048608 | tf_op jit(solution)/shard_map/ppermute | solution.py:10
  172.2 4.1 %convert_reduce_fusion = (f32[1024]{0:T(1024)}, bf16[512,1024]{1,0:T(8,128)(2,1)S(1)}) fusion(bf16[512,1024]{1,0:T(8,128)(2,1)} %collective-permute-done.1, bf16[512,1024]{1,0:T(8,128)(2,1)S(1)} %copy-done.1, bf16[1,2,512,1024]{3,2,1,0:T(8,128)(2,1)} %param.18, s32[]{:T(128)S(6)} %select_n.28, pred[]{:T(512)S(6)} %eq.20), kind=kLoop, calls=%fused_computation.46 | loop fusion | flops 14679040 | bytes 4198405 | tf_op jit(solution)/shard_map/reduce_sum | solution.py:73
  177.3 9.6 %fusion.14 = bf16[512,4096]{1,0:T(8,128)(2,1)} fusion(bf16[512,1024]{1,0:T(8,128)(2,1)S(1)} %get-tuple-element.77, bf16[1,4096,1024]{2,1,0:T(8,128)(2,1)} %param.19), kind=kOutput, calls=%fused_computation.19 | convolution fusion | flops 4297064448 | bytes 13631488 | tf_op jit(solution)/shard_map/dot_general | solution.py:87
  187.0 1.2 copy-done.3
  188.1 9.0 %convert_bitcast_fusion = bf16[1,4096,1024]{2,1,0:T(8,128)(2,1)} fusion(bf16[512,1024]{1,0:T(8,128)(2,1)S(1)} %copy-done.3, bf16[1,1,512,4096]{3,2,1,0:T(8,128)(2,1)} %all-gather.6.cloned.1.call-done), kind=kOutput, calls=%fused_computation.18 | convolution fusion | flops 4299161600 | bytes 13631488 | tf_op jit(solution)/shard_map/dot_general | solution.py:80
  197.1 10.7 %fusion.39 = bf16[1,512,1024]{2,1,0:T(8,128)(2,1)} fusion(bf16[512,4096]{1,0:T(8,128)(2,1)} %all-gather.4.cloned.1.call-done, bf16[1,4096,1024]{2,1,0:T(8,128)(2,1)} %param.19, f32[1024]{0:T(1024)S(1)} %bitcast.53), kind=kOutput, calls=%fused_computation.48 | convolution fusion | flops 4300210176 | bytes 13635584 | tf_op jit(solution)/shard_map/dot_general | solution.py:75
  207.8 23.1 %reduce-scatter.2.cloned.1.call-done = bf16[512,1024]{1,0:T(8,128)(2,1)} async-done(((bf16[512,4096]{1,0:T(8,128)(2,1)}), bf16[512,1024]{1,0:T(8,128)(2,1)}) %reduce-scatter.2.cloned.1.call-update) | async-done | bytes 1048592 | tf_op jit(solution)/shard_map/reduce_scatter | solution.py:90
  (35 shorter events, 8.9 us)
Async XLA Ops:
  8.0 63.7 %copy-start = (bf16[1,2,512,1024]{3,2,1,0:T(8,128)(2,1)S(1)}, bf16[1,2,512,1024]{3,2,1,0:T(8,128)(2,1)}, u32[]{:S(2)}) copy-start(bf16[1,2,512,1024]{3,2,1,0:T(8,128)(2,1)} %param.17) | copy-start | bytes 6291460
  8.0 132.6 %all-reduce.3.cloned.1.call-start = ((), (), s32[]{:S(2)}) async-start(), calls=%async_computation.1 | async-start | bytes 2097152 | tf_op jit(solution)/shard_map/psum | solution.py:57
  71.0 69.7 %copy-start.4 = (f32[2,1024]{1,0:T(2,128)S(1)}, f32[2,1024]{1,0:T(2,128)}, u32[]{:S(2)}) copy-start(f32[2,1024]{1,0:T(2,128)} %param.25) | copy-start | bytes 24580
  71.0 69.7 %copy-start.5 = (f32[512,2]{0,1:T(2,128)S(1)}, f32[512,2]{0,1:T(2,128)}, u32[]{:S(2)}) copy-start(f32[512,2]{0,1:T(2,128)} %param.24) | copy-start | bytes 12292
  71.0 116.0 %all-gather.6.cloned.1.call-start = ((), (), s32[]{:S(2)}) async-start(), calls=%async_computation.4 | async-start | bytes 5242880 | tf_op jit(solution)/shard_map/all_gather | solution.py:81
  72.9 124.2 %all-gather.4.cloned.1.call-start = ((), (), s32[]{:S(2)}) async-start(), calls=%async_computation.2 | async-start | bytes 5242880 | tf_op jit(solution)/shard_map/all_gather | solution.py:76
  72.9 44.5 %collective-permute-start = (bf16[512,1024]{1,0:T(8,128)(2,1)}, bf16[512,1024]{1,0:T(8,128)(2,1)}, u32[]{:S(2)}, u32[]{:S(2)}) collective-permute-start(bf16[512,1024]{1,0:T(8,128)(2,1)} %bitcast.1), channel_id=1, source_target_pairs={{0,4},{4,8},{8,12},{1,5},{5,9},{9,13},{2,6},{6,10},{10,14},{3,7},{... | collective-permute-start | bytes 3145736 | tf_op jit(solution)/shard_map/ppermute | solution.py:10
  78.8 93.4 %copy-start.1 = (bf16[512,1024]{1,0:T(8,128)(2,1)S(1)}, bf16[512,1024]{1,0:T(8,128)(2,1)}, u32[]{:S(2)}) copy-start(bf16[512,1024]{1,0:T(8,128)(2,1)} %param.26) | copy-start | bytes 3145732
  144.9 86.0 %reduce-scatter.2.cloned.1.call-start = ((), (), s32[]{:S(2)}) async-start(), calls=%async_computation.3 | async-start | bytes 5242880 | tf_op jit(solution)/shard_map/reduce_scatter | solution.py:90
  144.9 27.3 %collective-permute-start.1 = (bf16[512,1024]{1,0:T(8,128)(2,1)}, bf16[512,1024]{1,0:T(8,128)(2,1)}, u32[]{:S(2)}, u32[]{:S(2)}) collective-permute-start(bf16[512,1024]{1,0:T(8,128)(2,1)} %bitcast.51), channel_id=1, source_target_pairs={{4,0},{8,4},{12,8},{5,1},{9,5},{13,9},{6,2},{10,6},{14,10},{7,3},{... | collective-permute-start | bytes 3145736 | tf_op jit(solution)/shard_map/ppermute | solution.py:10
  176.3 1.0 copy-start.2
  186.9 1.2 copy-start.3
  186.9 10.2 %copy-start.6 = (f32[1,1024]{1,0:T(1,128)S(1)}, f32[1,1024]{1,0:T(1,128)}, u32[]{:S(2)}) copy-start(f32[1,1024]{1,0:T(1,128)} %param.20) | copy-start | bytes 12292
Sparse Core Ops, SparseCore 0:
  71.1 69.4 all-reduce.2
Sparse Core Ops, SparseCore 1:
  73.0 37.0 all-gather.5
  144.9 34.0 all-gather.3
  187.0 43.8 reduce-scatter.1
where the time goes:
time: 239 us; the launch traced here: 238 us
  waiting for transfers between devices  111 us (46%)
  matrix products  56.4 us (24%)
  other arithmetic  36.4 us (15%)
  between operations  16.4 us (7%)
  local copies, waits for them, and re-layouts  10.8 us (5%)
  starting transfers between devices  7.57 us (3%)
    ppermute x2, waiting for transfers between devices, from_behind(): return lax.ppermute(shard, axis, pairs)  64.4 us
    reduce_sum x3, other arithmetic, add_block(): amplitude = jnp.sum(jnp.where(matched, seg_amp[:, :, None], 0.0), axis=1)  26.9 us
    psum x1, waiting for transfers between devices, local(): lax.psum(partial_value.astype(jnp.bfloat16), 'section').astype(jnp.float32)  23.2 us
    reduce_scatter x1, waiting for transfers between devices, local(): lax.psum_scatter(partial_terms.astype(jnp.bfloat16), 'fsdp', scatter_dime...  23.1 us
    dot_general x3, matrix products, add_block(): jnp.dot(lower, table_block, preferred_element_type=jnp.float32)  13.2 us
    dot_general x1, matrix products, local(): jnp.dot(lax.all_gather(layer_input, 'fsdp', axis=1, tiled=True), weight,...  10.7 us
    dot_general x3, matrix products, add_block(): jnp.dot(upper, table_block, preferred_element_type=jnp.float32)  9.82 us
    dot_general x1, matrix products, local(): lax.dot_general(pre_grad, weight, (((1,), (1,)), ((), ())), preferred_ele...  9.61 us
  transfers between devices with their start and end apart: 6, of which 4 were waited for; matrix products, arithmetic and copies ran while one was open for 16% of the time, Pallas kernels for 0%

commit v1 on v0

--- a/solution.py
+++ b/solution.py
@@ -1,6 +1,8 @@
 import jax
 import jax.numpy as jnp
 from jax import lax
+from jax.experimental import pallas as pl
+from jax.experimental.pallas import tpu as pltpu
 from jax.sharding import PartitionSpec as P
 
 
@@ -10,30 +12,46 @@
     return lax.ppermute(shard, axis, pairs)
 
 
-def lookup_sum(full_table, seg_index, seg_amp, first_row):
-    row_count = full_table.shape[0]
-    feature_count = full_table.shape[1]
-    block_rows = 512
-    block_count = (row_count + block_rows - 1) // block_rows
-    padded = jnp.pad(full_table, ((0, block_count * block_rows - row_count), (0, 0)))
-    blocks = padded.reshape(block_count, block_rows, feature_count)
-    starts = jnp.arange(block_count, dtype=jnp.int32) * block_rows
-    local_row = seg_index - first_row
+def embed_rows(row_block, local_ref, amp_ref, matrix_ref):
+    begin = pl.multiple_of(row_block * 16, 16)
+    wide = matrix_ref.shape[1]
+    ids = local_ref[pl.ds(begin, 16), :]
+    amps = amp_ref[pl.ds(begin, 16), :]
+    position = lax.broadcasted_iota(jnp.int32, (16, wide), 1)
+    total = jnp.zeros((16, wide), jnp.float32)
+    for k in range(local_ref.shape[1]):
+        total = total + jnp.where(ids[:, k : k + 1] == position, amps[:, k : k + 1], 0.0)
+    matrix_ref[pl.ds(begin, 16), :] = total.astype(jnp.bfloat16)
 
-    def add_block(total, item):
-        table_block, start = item
-        position = start + jnp.arange(block_rows, dtype=jnp.int32)
-        matched = local_row[:, :, None] == position[None, None, :]
-        amplitude = jnp.sum(jnp.where(matched, seg_amp[:, :, None], 0.0), axis=1)
-        upper = amplitude.astype(jnp.bfloat16)
-        lower = (amplitude - upper.astype(jnp.float32)).astype(jnp.bfloat16)
-        total = total + jnp.dot(upper, table_block, preferred_element_type=jnp.float32)
-        total = total + jnp.dot(lower, table_block, preferred_element_type=jnp.float32)
-        return (total, None)
 
-    empty = jnp.zeros((seg_index.shape[0], feature_count), jnp.float32)
-    summed, unused = lax.scan(add_block, empty, (blocks, starts))
-    return summed
+def embed_kernel(local_ref, amp_ref, table_ref, out_ref, matrix_ref):
+    rows = table_ref.shape[0]
+
+    def step(row_block, carry):
+        embed_rows(row_block, local_ref, amp_ref, matrix_ref)
+        return carry
+
+    lax.fori_loop(0, local_ref.shape[0] // 16, step, 0)
+    out_ref[...] = jnp.dot(
+        matrix_ref[:, :rows], table_ref[...], preferred_element_type=jnp.float32
+    ).astype(jnp.bfloat16)
+
+
+def lookup_sum(table, seg_index, seg_amp, first_row):
+    samples = seg_index.shape[0]
+    rows, width = table.shape
+    wide = (rows + 127) // 128 * 128
+    return pl.pallas_call(
+        embed_kernel,
+        out_shape=jax.ShapeDtypeStruct((samples, width), jnp.bfloat16),
+        in_specs=[pl.BlockSpec(memory_space=pltpu.VMEM)] * 3,
+        out_specs=pl.BlockSpec(memory_space=pltpu.VMEM),
+        scratch_shapes=[pltpu.VMEM((samples, wide), jnp.bfloat16)],
+        compiler_params=pltpu.CompilerParams(vmem_limit_bytes=32 * 1024 * 1024),
+        cost_estimate=pl.CostEstimate(
+            flops=2 * samples * rows * width, bytes_accessed=4 * rows * width, transcendentals=0
+        ),
+    )(seg_index - first_row, seg_amp, table)
 
 
 def local(

time: 239 us -> 195 us (0.82)
  other arithmetic: 36.4 us -> 4.1 us
  matrix products: 56.4 us -> 33.4 us
  Pallas kernels: 0 us -> 15.3 us
  local copies, waits for them, and re-layouts: 10.8 us -> 7.03 us
    ppermute x2, waiting for transfers between devices: 64.4 us -> 25.8 us  [from_behind(): return lax.ppermute(shard, axis, pairs)]
    psum x1, waiting for transfers between devices: 23.2 us -> 61.8 us  [local(): lax.psum(partial_value.astype(jnp.bfloat16), 'section').astype(jnp.float32)]
    reduce_sum x3 -> x0, other arithmetic: 26.9 us -> none  [add_block(): amplitude = jnp.sum(jnp.where(matched, seg_amp[:, :, None], 0.0), axis=1)]
    dot_general x6 -> x0, matrix products: 23 us -> none  [the longest x3 13.2 us: add_block(): jnp.dot(lower, table_block, preferred_element_type=jnp.float32)]
    pallas_call x0 -> x1, Pallas kernels: none -> 15.3 us  [lookup_sum(): pl.pallas_call(embed_kernel, out_shape=jax.ShapeDtypeStruct((samples, wid...]
    pad x1 -> x0, local copies, waits for them, and re-layouts: 3.71 us -> none  [lookup_sum(): jnp.pad(full_table, ((0, block_count * block_rows - row_count), (0, 0)))]
    convert_element_type x1 -> x0, other arithmetic: 2.72 us -> none  [local(): partial_value.astype(jnp.bfloat16)]
    unnamed x16 -> x18, local copies, waits for them, and re-layouts: 4.21 us -> 5.9 us
  transfers between devices with their start and end apart: 6 -> 6, of which waited for: 4 -> 3; matrix products, arithmetic and copies ran while one was open for 16% -> 20% of each run, Pallas kernels for 0% -> 0%
where the time goes in v1:
time: 195 us
  waiting for transfers between devices  111 us (57%)
  matrix products  33.4 us (17%)
  between operations  16.4 us (8%)
  Pallas kernels  15.3 us (8%)
  starting transfers between devices  7.59 us (4%)
  local copies, waits for them, and re-layouts  7.03 us (4%)
  other arithmetic  4.1 us (2%)
    psum x1, waiting for transfers between devices, local(): lax.psum(partial_value.astype(jnp.bfloat16), 'section').astype(jnp.float32)  61.8 us
    ppermute x2, waiting for transfers between devices, from_behind(): return lax.ppermute(shard, axis, pairs)  25.8 us
    reduce_scatter x1, waiting for transfers between devices, local(): lax.psum_scatter(partial_terms.astype(jnp.bfloat16), 'fsdp', scatter_dime...  23.1 us
    pallas_call x1, Pallas kernels, lookup_sum(): pl.pallas_call(embed_kernel, out_shape=jax.ShapeDtypeStruct((samples, wid...  15.3 us
    dot_general x1, matrix products, local(): jnp.dot(lax.all_gather(layer_input, 'fsdp', axis=1, tiled=True), weight,...  10.7 us
    dot_general x1, matrix products, local(): lax.dot_general(pre_grad, weight, (((1,), (1,)), ((), ())), preferred_ele...  9.61 us
    dot_general x1, matrix products, local(): lax.dot_general(lax.all_gather(stashed_in, 'fsdp', axis=1, tiled=True), p...  8.98 us
    ppermute x2, starting transfers between devices, from_behind(): return lax.ppermute(shard, axis, pairs)  7.42 us
  transfers between devices with their start and end apart: 6, of which 3 were waited for; matrix products, arithmetic and copies ran while one was open for 20% of the time, Pallas kernels for 0%

profile of v1, /device:TPU:0, one launch (start us, length us, event | category | flops | bytes accessed | tf_op | source)
XLA Modules:
  0.0 194.7 jit_solution(5509366788502381837)
XLA Ops:
  8.0 0.0 all-reduce.2.cloned.1.call-start
  8.1 1.1 copy.19
  9.2 1.0 copy.21.amp_ref
  10.2 1.7 copy-done.1
  11.9 15.3 %shard_map.156 = bf16[512,1024]{1,0:T(8,128)(2,1)} custom-call(s32[512,32]{1,0:T(8,128)S(1)} %broadcast_subtract_fusion.local_ref, f32[512,32]{1,0:T(8,128)S(1)} %copy.21.amp_ref, bf16[1196,1024]{1,0:T(8,128)(2,1)S(1)} %copy-done.1), custom_call_target="tpu_custom_call" | custom-call | flops 1254096896 | bytes 4898816 | tf_op jit(solution)/shard_map/pallas_call | solution.py:44
  27.2 0.0 all-gather.6.cloned.1.call-start
  27.9 1.1 constant_dynamic-slice_fusion
  29.1 0.0 all-gather.6.cloned.1.call-update
  29.1 0.0 all-gather.4.cloned.1.call-start
  29.1 6.0 %collective-permute-start = (bf16[512,1024]{1,0:T(8,128)(2,1)}, bf16[512,1024]{1,0:T(8,128)(2,1)}, u32[]{:S(2)}, u32[]{:S(2)}) collective-permute-start(bf16[512,1024]{1,0:T(8,128)(2,1)} %bitcast), channel_id=1, source_target_pairs={{0,4},{4,8},{8,12},{1,5},{5,9},{9,13},{2,6},{6,10},{10,14},{3,7},{... | collective-permute-start | bytes 3145736 | tf_op jit(solution)/shard_map/ppermute | solution.py:12
  35.1 61.8 %all-reduce.2.cloned.1.call-done = bf16[512,1024]{1,0:T(8,128)(2,1)} async-done(((bf16[512,1024]{1,0:T(8,128)(2,1)}), bf16[512,1024]{1,0:T(8,128)(2,1)}) %all-reduce.2.cloned.1.call-update) | async-done | bytes 1048592 | tf_op jit(solution)/shard_map/psum | solution.py:75
  96.9 4.2 %fusion.32 = bf16[512,1024]{1,0:T(8,128)(2,1)} fusion(bf16[512,1024]{1,0:T(8,128)(2,1)} %collective-permute-done, f32[512,2]{0,1:T(2,128)S(1)} %copy-done.6, f32[2,1024]{1,0:T(2,128)S(1)} %copy-done.5, bf16[512,1024]{1,0:T(8,128)(2,1)} %all-reduce.2.cloned.1.call-done, pred[]{:T(512)S(6)} %eq.6), kind=kOutput, calls=%fused_computation.35 | convolution fusion | flops 14680064 | bytes 3158017 | tf_op jit(solution)/shard_map/dot_general | solution.py:76
  101.1 0.0 all-gather.4.cloned.1.call-update
  101.1 0.0 reduce-scatter.2.cloned.1.call-start
  101.1 1.5 collective-permute-start.1
  102.6 25.8 %collective-permute-done.1 = bf16[512,1024]{1,0:T(8,128)(2,1)} collective-permute-done((bf16[512,1024]{1,0:T(8,128)(2,1)}, bf16[512,1024]{1,0:T(8,128)(2,1)}, u32[]{:S(2)}, u32[]{:S(2)}) %collective-permute-start.1) | collective-permute-done | bytes 1048608 | tf_op jit(solution)/shard_map/ppermute | solution.py:12
  128.5 4.1 %convert_reduce_fusion = (f32[1024]{0:T(1024)}, bf16[512,1024]{1,0:T(8,128)(2,1)S(1)}) fusion(bf16[512,1024]{1,0:T(8,128)(2,1)} %collective-permute-done.1, bf16[512,1024]{1,0:T(8,128)(2,1)S(1)} %copy-done.2, bf16[1,2,512,1024]{3,2,1,0:T(8,128)(2,1)} %param.16, s32[]{:T(128)S(6)} %select_n.24, pred[]{:T(512)S(6)} %eq.7), kind=kLoop, calls=%fused_computation.32 | loop fusion | flops 14679040 | bytes 4198405 | tf_op jit(solution)/shard_map/reduce_sum | solution.py:91
  132.6 1.0 copy-done.3
  133.5 9.6 %fusion.4 = bf16[512,4096]{1,0:T(8,128)(2,1)} fusion(bf16[512,1024]{1,0:T(8,128)(2,1)S(1)} %get-tuple-element.5, bf16[1,4096,1024]{2,1,0:T(8,128)(2,1)} %param.17), kind=kOutput, calls=%fused_computation.5 | convolution fusion | flops 4297064448 | bytes 13631488 | tf_op jit(solution)/shard_map/dot_general | solution.py:105
  143.2 0.0 all-gather.6.cloned.1.call-done
  143.2 1.2 copy-done.4
  144.4 9.0 %convert_bitcast_fusion = bf16[1,4096,1024]{2,1,0:T(8,128)(2,1)} fusion(bf16[512,1024]{1,0:T(8,128)(2,1)S(1)} %copy-done.4, bf16[1,1,512,4096]{3,2,1,0:T(8,128)(2,1)} %all-gather.6.cloned.1.call-done), kind=kOutput, calls=%fused_computation.4 | convolution fusion | flops 4299161600 | bytes 13631488 | tf_op jit(solution)/shard_map/dot_general | solution.py:98
  153.3 10.7 %fusion.29 = bf16[1,512,1024]{2,1,0:T(8,128)(2,1)} fusion(bf16[512,4096]{1,0:T(8,128)(2,1)} %all-gather.4.cloned.1.call-done, bf16[1,4096,1024]{2,1,0:T(8,128)(2,1)} %param.17, f32[1024]{0:T(1024)S(1)} %bitcast.39), kind=kOutput, calls=%fused_computation.34 | convolution fusion | flops 4300210176 | bytes 13635584 | tf_op jit(solution)/shard_map/dot_general | solution.py:93
  164.0 23.1 %reduce-scatter.2.cloned.1.call-done = bf16[512,1024]{1,0:T(8,128)(2,1)} async-done(((bf16[512,4096]{1,0:T(8,128)(2,1)}), bf16[512,1024]{1,0:T(8,128)(2,1)}) %reduce-scatter.2.cloned.1.call-update) | async-done | bytes 1048592 | tf_op jit(solution)/shard_map/reduce_scatter | solution.py:108
  (18 shorter events, 0.1 us)
Async XLA Ops:
  8.0 19.9 %copy-start = (bf16[1,2,512,1024]{3,2,1,0:T(8,128)(2,1)S(1)}, bf16[1,2,512,1024]{3,2,1,0:T(8,128)(2,1)}, u32[]{:S(2)}) copy-start(bf16[1,2,512,1024]{3,2,1,0:T(8,128)(2,1)} %param.15) | copy-start | bytes 6291460
  8.0 88.9 %all-reduce.2.cloned.1.call-start = ((), (), s32[]{:S(2)}) async-start(), calls=%async_computation.1 | async-start | bytes 2097152 | tf_op jit(solution)/shard_map/psum | solution.py:75
  10.2 1.7 copy-start.1
  27.2 69.7 %copy-start.5 = (f32[2,1024]{1,0:T(2,128)S(1)}, f32[2,1024]{1,0:T(2,128)}, u32[]{:S(2)}) copy-start(f32[2,1024]{1,0:T(2,128)} %param.23) | copy-start | bytes 24580
  27.2 69.7 %copy-start.6 = (f32[512,2]{0,1:T(2,128)S(1)}, f32[512,2]{0,1:T(2,128)}, u32[]{:S(2)}) copy-start(f32[512,2]{0,1:T(2,128)} %param.22) | copy-start | bytes 12292
  27.2 116.0 %all-gather.6.cloned.1.call-start = ((), (), s32[]{:S(2)}) async-start(), calls=%async_computation.4 | async-start | bytes 5242880 | tf_op jit(solution)/shard_map/all_gather | solution.py:99
  29.1 124.3 %all-gather.4.cloned.1.call-start = ((), (), s32[]{:S(2)}) async-start(), calls=%async_computation.2 | async-start | bytes 5242880 | tf_op jit(solution)/shard_map/all_gather | solution.py:94
  29.1 67.7 %collective-permute-start = (bf16[512,1024]{1,0:T(8,128)(2,1)}, bf16[512,1024]{1,0:T(8,128)(2,1)}, u32[]{:S(2)}, u32[]{:S(2)}) collective-permute-start(bf16[512,1024]{1,0:T(8,128)(2,1)} %bitcast), channel_id=1, source_target_pairs={{0,4},{4,8},{8,12},{1,5},{5,9},{9,13},{2,6},{6,10},{10,14},{3,7},{... | collective-permute-start | bytes 3145736 | tf_op jit(solution)/shard_map/ppermute | solution.py:12
  35.1 93.4 %copy-start.2 = (bf16[512,1024]{1,0:T(8,128)(2,1)S(1)}, bf16[512,1024]{1,0:T(8,128)(2,1)}, u32[]{:S(2)}) copy-start(bf16[512,1024]{1,0:T(8,128)(2,1)} %param.24) | copy-start | bytes 3145732
  101.1 86.0 %reduce-scatter.2.cloned.1.call-start = ((), (), s32[]{:S(2)}) async-start(), calls=%async_computation.3 | async-start | bytes 5242880 | tf_op jit(solution)/shard_map/reduce_scatter | solution.py:108
  101.1 27.3 %collective-permute-start.1 = (bf16[512,1024]{1,0:T(8,128)(2,1)}, bf16[512,1024]{1,0:T(8,128)(2,1)}, u32[]{:S(2)}, u32[]{:S(2)}) collective-permute-start(bf16[512,1024]{1,0:T(8,128)(2,1)} %bitcast.37), channel_id=1, source_target_pairs={{4,0},{8,4},{12,8},{5,1},{9,5},{13,9},{6,2},{10,6},{14,10},{7,3},{... | collective-permute-start | bytes 3145736 | tf_op jit(solution)/shard_map/ppermute | solution.py:12
  132.6 1.0 copy-start.3
  143.1 1.2 copy-start.4
  143.2 10.2 %copy-start.7 = (f32[1,1024]{1,0:T(1,128)S(1)}, f32[1,1024]{1,0:T(1,128)}, u32[]{:S(2)}) copy-start(f32[1,1024]{1,0:T(1,128)} %param.18) | copy-start | bytes 12292
Sparse Core Ops, SparseCore 0:
  27.3 69.4 all-reduce.1
Sparse Core Ops, SparseCore 1:
  29.3 37.0 all-gather.5
  101.2 34.0 all-gather.3
  143.2 43.8 reduce-scatter.1

commit v2 on v0

v2 whole, which is shorter than its diff:
```python
import functools

import jax
import jax.numpy as jnp
from jax import lax
from jax.experimental import pallas as pl
from jax.experimental.pallas import tpu as pltpu
from jax.sharding import PartitionSpec as P

CHUNKS = 4
MESH = pl.DeviceIdType.MESH
ROOT = 0.7978845608028654
CUBIC = 0.044715


def gelu_parts(x):
    squared = x * x
    t = jnp.tanh(ROOT * (x + CUBIC * x * squared))
    half = 0.5 * (1.0 + t)
    slope = half + 0.5 * x * (1.0 - t * t) * (ROOT * (1.0 + 3.0 * CUBIC * squared))
    return x * half, slope


def gelu(x):
    return x * (0.5 * (1.0 + jnp.tanh(ROOT * (x + CUBIC * x * x * x))))


def kernel(
    sections, shards,
    act_hbm, grad_hbm, stash_ref, pre_ref, weight_hbm, bias_ref, table_ref, index_ref, amp_ref,
    field_ref, angle_ref, target_ref, sched_ref,
    fwd_ref, grad_in_ref, grad_w_hbm, grad_bias_ref,
    weight, feat, stash, from_next, matrix, emb, emb_recv, emb_send, pre_grad,
    part_send, part_recv, own, x_recv, grad_w,
    load_sem, z_send, z_recv, near_send, near_recv, far_send, far_recv, pass_send, pass_recv,
    part_send_sem, part_recv_sem, sum_send_sem, sum_recv_sem, store_sem,
):
    me = lax.axis_index("fsdp")
    sec = lax.axis_index("section")
    chips = shards // 2
    chip, core = me // 2, lax.rem(me, 2)
    partner = chip * 2 + 1 - core
    rows, width = pre_grad.shape
    part = rows // CHUNKS
    tile = min(256, width)

    def at_chip(j, c):
        return lax.rem(chip + j, chips) * 2 + c

    def span(c):
        return pl.ds(c * part, part)

    def remote(src, dst, send, recv, **where):
        return pltpu.make_async_remote_copy(
            src_ref=src, dst_ref=dst, send_sem=send, recv_sem=recv,
            device_id=where, device_id_type=MESH,
        )

    not_last = sec < sections - 1
    not_first = sec > 0

    load = pltpu.make_async_copy(weight_hbm.at[0], weight, load_sem)
    load.start()

    barrier = pltpu.get_barrier_semaphore()
    pl.semaphore_signal(barrier, inc=1, device_id={"fsdp": partner}, device_id_type=MESH)
    for j in range(1, chips):
        pl.semaphore_signal(barrier, inc=1, device_id={"fsdp": at_chip(j, core)}, device_id_type=MESH)

    @pl.when(not_last)
    def _():
        pl.semaphore_signal(barrier, inc=1, device_id={"section": sec + 1}, device_id_type=MESH)

    @pl.when(not_first)
    def _():
        pl.semaphore_signal(barrier, inc=1, device_id={"section": sec - 1}, device_id_type=MESH)

    pl.semaphore_wait(barrier, chips + jnp.where(not_last, 1, 0) + jnp.where(not_first, 1, 0))

    def act_copy(c):
        return remote(act_hbm.at[0, span(c)], feat.at[me, span(c)], z_send.at[0, c], z_recv.at[0, c], section=sec + 1)

    def grad_copy(c):
        return remote(grad_hbm.at[0, span(c)], from_next.at[span(c)], z_send.at[1, c], z_recv.at[1, c], section=sec - 1)

    def emb_copy(c):
        return remote(emb_send.at[span(c)], emb_recv.at[span(c)], z_send.at[2, c], z_recv.at[2, c], section=sec - 1)

    @pl.when(not_first)
    def _():
        for c in range(CHUNKS):
            grad_copy(c).start()

    @pl.when(not_last)
    def _():
        for c in range(CHUNKS):
            act_copy(c).start()

    def near_copy(g, buf, c, block):
        return remote(buf.at[block, span(c)], buf.at[block, span(c)], near_send.at[g, c], near_recv.at[g, c], fsdp=partner)

    def far_copy(g, buf, c, j, block):
        return remote(buf.at[block, span(c)], buf.at[block, span(c)], far_send.at[g, c, j - 1], far_recv.at[g, c, j - 1], fsdp=at_chip(j, core))

    def pass_copy(g, buf, c, j, block):
        return remote(buf.at[block, span(c)], buf.at[block, span(c)], pass_send.at[g, c, j - 1], pass_recv.at[g, c, j - 1], fsdp=partner)

    def gather_start(g, buf, c):
        for j in range(1, chips):
            far_copy(g, buf, c, j, me).start()
        near_copy(g, buf, c, me).start()

    def gather_pass(g, buf, c):
        for j in range(1, chips):
            block = at_chip(chips - j, core)
            far_copy(g, buf, c, j, block).wait_recv()
            pass_copy(g, buf, c, j, block).start()

    def gather_end(g, buf, c):
        near_copy(g, buf, c, partner).wait_recv()
        for j in range(1, chips):
            pass_copy(g, buf, c, j, at_chip(chips - j, 1 - core)).wait_recv()

    def gather_drain(g, buf, c):
        near_copy(g, buf, c, me).wait_send()
        for j in range(1, chips):
            far_copy(g, buf, c, j, me).wait_send()
            pass_copy(g, buf, c, j, at_chip(chips - j, core)).wait_send()

    slot = sched_ref[0]
    for c in range(CHUNKS):
        stash[me, span(c), :] = jnp.where(slot == 0, stash_ref[0, 0, span(c), :], stash_ref[0, 1, span(c), :])
        gather_start(0, stash, c)

    table_rows = table_ref.shape[0]
    wide = matrix.shape[1]
    base = sec * table_rows

    def amplitudes(i, carry):
        begin = pl.multiple_of(i * 16, 16)
        ids = index_ref[pl.ds(begin, 16), :]
        amps = amp_ref[pl.ds(begin, 16), :]
        position = lax.broadcasted_iota(jnp.int32, (16, wide), 1) + base
        total = jnp.zeros((16, wide), jnp.float32)
        for k in range(index_ref.shape[1]):
            total = total + jnp.where(ids[:, k : k + 1] == position, amps[:, k : k + 1], 0.0)
        matrix[pl.ds(begin, 16), :] = total.astype(jnp.bfloat16)
        return carry

    for c in range(CHUNKS):
        lax.fori_loop(c * part // 16, (c + 1) * part // 16, amplitudes, 0)
        emb[span(c), :] = jnp.dot(
            matrix[span(c), :table_rows], table_ref[...], preferred_element_type=jnp.float32
        )

        @pl.when(jnp.logical_not(not_last))
        def _():
            emb_send[span(c), :] = emb[span(c), :].astype(jnp.bfloat16)
            emb_copy(c).start()

    grad_bias_ref[...] = jnp.zeros_like(grad_bias_ref)
    for c in range(CHUNKS):
        @pl.when(not_last)
        def _():
            grad_copy(c).wait_recv()

        def backward(i, carry):
            at = pl.ds(pl.multiple_of(c * part + i * 16, 16), 16)
            saved = jnp.where(slot == 0, pre_ref[0, 0, at, :], pre_ref[0, 1, at, :]).astype(jnp.float32)
            value, slope = gelu_parts(saved)
            cotangent = jnp.where(
                not_last, from_next[at, :].astype(jnp.float32), value - target_ref[at, :].astype(jnp.float32)
            )
            result = (cotangent * slope).astype(jnp.bfloat16)
            pre_grad[at, :] = result
            grad_bias_ref[...] += jnp.sum(result.astype(jnp.float32), axis=0, keepdims=True)
            return carry

        lax.fori_loop(0, part // 16, backward, 0)

        @pl.when(not_first)
        def _():
            act_copy(c).wait_recv()
            gather_start(1, feat, c)

    load.wait()

    def input_part(j, c, into):
        block = at_chip(j, c)

        def step(t, carry):
            begin = pl.multiple_of(block * width + t * tile, tile)
            column = pl.ds(pl.multiple_of(t * tile, tile), tile)
            into[j, :, column] = lax.dot_general(
                pre_grad[...], weight[pl.ds(begin, tile), :], (((1,), (1,)), ((), ())),
                preferred_element_type=jnp.float32,
            ).astype(jnp.bfloat16)
            return carry

        lax.fori_loop(0, width // tile, step, 0)

    def part_copy(j):
        return remote(part_send.at[j], part_recv.at[j], part_send_sem.at[j], part_recv_sem.at[j], fsdp=partner)

    def sum_copy(j):
        return remote(own.at[j], x_recv.at[j - 1], sum_send_sem.at[j - 1], sum_recv_sem.at[j - 1], fsdp=at_chip(j, core))

    def chain(c):
        @pl.when(not_last)
        def _():
            emb_copy(c).wait_recv()

            def add(i, carry):
                at = pl.ds(pl.multiple_of(c * part + i * 16, 16), 16)
                total = emb[at, :] + emb_recv[at, :].astype(jnp.float32)

                @pl.when(not_first)
                def _():
                    emb_send[at, :] = total.astype(jnp.bfloat16)

                @pl.when(sec == 0)
                def _():
                    angular = (
                        field_ref[at, 0:1] * angle_ref[0:1, :] + field_ref[at, 1:2] * angle_ref[1:2, :]
                    )
                    feat[me, at, :] = (total + angular).astype(jnp.bfloat16)

                return carry

            lax.fori_loop(0, part // 16, add, 0)

            @pl.when(not_first)
            def _():
                emb_copy(c).start()

            @pl.when(sec == 0)
            def _():
                gather_start(1, feat, c)

    for j in range(1, chips):
        input_part(j, 1 - core, part_send)
        part_copy(j).start()
    for j in range(1, chips):
        input_part(j, core, own)
        part_copy(j).wait_recv()
        for c in range(CHUNKS):
            own[j, span(c), :] = (
                own[j, span(c), :].astype(jnp.float32) + part_recv[j, span(c), :].astype(jnp.float32)
            ).astype(jnp.bfloat16)
        sum_copy(j).start()
    chain(0)
    input_part(0, 1 - core, part_send)
    part_copy(0).start()
    chain(1)
    input_part(0, core, own)
    chain(2)

    def store_copy(block):
        at = pl.ds(pl.multiple_of(block * width, width), width)
        return pltpu.make_async_copy(grad_w.at[at, :], grad_w_hbm.at[0, at, :], store_sem.at[block])

    def weight_grad(block):
        def step(t, carry):
            begin = pl.multiple_of(block * width + t * tile, tile)
            column = pl.ds(pl.multiple_of(t * tile, tile), tile)
            grad_w[pl.ds(begin, tile), :] = lax.dot_general(
                stash[block, :, column], pre_grad[...], (((0,), (0,)), ((), ())),
                preferred_element_type=jnp.float32,
            ).astype(jnp.bfloat16)
            return carry

        lax.fori_loop(0, width // tile, step, 0)
        store_copy(block).start()

    for c in range(CHUNKS):
        gather_pass(0, stash, c)
    weight_grad(me)
    chain(3)
    for c in range(CHUNKS):
        gather_end(0, stash, c)
    weight_grad(partner)
    for j in range(1, chips):
        weight_grad(at_chip(j, core))
        weight_grad(at_chip(j, 1 - core))

    def forward(c):
        total = jnp.zeros((part, width), jnp.float32)
        for b in range(shards):
            total = total + jnp.dot(
                feat[b, span(c), :], weight[b * width : (b + 1) * width, :],
                preferred_element_type=jnp.float32,
            )
        fwd_ref[0, span(c), :] = gelu(total + bias_ref[...]).astype(jnp.bfloat16)

    for c in range(CHUNKS):
        gather_pass(1, feat, c)
        if c > 0:
            gather_end(1, feat, c - 1)
            forward(c - 1)
    gather_end(1, feat, CHUNKS - 1)
    forward(CHUNKS - 1)

    part_copy(0).wait_recv()
    for j in range(1, chips):
        sum_copy(j).wait_recv()
    for c in range(CHUNKS):
        total = own[0, span(c), :].astype(jnp.float32) + part_recv[0, span(c), :].astype(jnp.float32)
        for j in range(1, chips):
            total = total + x_recv[j - 1, span(c), :].astype(jnp.float32)
        grad_in_ref[0, span(c), :] = total.astype(jnp.bfloat16)

    for c in range(CHUNKS):
        gather_drain(0, stash, c)
        gather_drain(1, feat, c)
    for j in range(chips):
        part_copy(j).wait_send()
    for j in range(1, chips):
        sum_copy(j).wait_send()
    for b in range(shards):
        store_copy(b).wait()

    @pl.when(not_last)
    def _():
        for c in range(CHUNKS):
            act_copy(c).wait_send()

    @pl.when(not_first)
    def _():
        for c in range(CHUNKS):
            grad_copy(c).wait_send()
            emb_copy(c).wait_send()


def local(sections, shards, *args):
    rows, width = args[0].shape[1:]
    table_rows = args[6].shape[0]
    wide = (table_rows + 127) // 128 * 128
    chips = shards // 2
    vmem = pl.BlockSpec(memory_space=pltpu.VMEM)
    hbm = pl.BlockSpec(memory_space=pl.ANY)
    smem = pl.BlockSpec(memory_space=pltpu.SMEM)
    dma = pltpu.SemaphoreType.DMA
    half, full = jnp.bfloat16, jnp.float32
    return pl.pallas_call(
        functools.partial(kernel, sections, shards),
        out_shape=(
            jax.ShapeDtypeStruct((1, rows, width), half),
            jax.ShapeDtypeStruct((1, rows, width), half),
            jax.ShapeDtypeStruct((1, shards * width, width), half),
            jax.ShapeDtypeStruct((1, width), full),
        ),
        in_specs=[hbm, hbm, vmem, vmem, hbm] + [vmem] * 7 + [smem],
        out_specs=(vmem, vmem, hbm, vmem),
        scratch_shapes=[
            pltpu.VMEM((shards * width, width), half),
            pltpu.VMEM((shards, rows, width), half),
            pltpu.VMEM((shards, rows, width), half),
            pltpu.VMEM((rows, width), half),
            pltpu.VMEM((rows, wide), half),
            pltpu.VMEM((rows, width), full),
            pltpu.VMEM((rows, width), half),
            pltpu.VMEM((rows, width), half),
            pltpu.VMEM((rows, width), half),
            pltpu.VMEM((chips, rows, width), half),
            pltpu.VMEM((chips, rows, width), half),
            pltpu.VMEM((chips, rows, width), half),
            pltpu.VMEM((chips - 1, rows, width), half),
            pltpu.VMEM((shards * width, width), half),
            dma,
            dma((3, CHUNKS)),
            dma((3, CHUNKS)),
            dma((2, CHUNKS)),
            dma((2, CHUNKS)),
            dma((2, CHUNKS, chips - 1)),
            dma((2, CHUNKS, chips - 1)),
            dma((2, CHUNKS, chips - 1)),
            dma((2, CHUNKS, chips - 1)),
            dma((chips,)),
            dma((chips,)),
            dma((chips - 1,)),
            dma((chips - 1,)),
            dma((shards,)),
        ],
        compiler_params=pltpu.CompilerParams(
            collective_id=0, has_side_effects=True, vmem_limit_bytes=60 * 1024 * 1024
        ),
        cost_estimate=pl.CostEstimate(
            flops=6 * rows * shards * width * width, bytes_accessed=40 * rows * width, transcendentals=0
        ),
    )(*args)


def solution(mesh):
    return jax.shard_map(
        functools.partial(local, mesh.shape["section"], mesh.shape["fsdp"]),
        mesh=mesh,
        in_specs=(
            P("section", "groups", "fsdp"),
            P("section", "groups", "fsdp"),
            P("section", None, "groups", "fsdp"),
            P("section", None, "groups", "fsdp"),
            P("section", None, "fsdp"),
            P("section", "fsdp"),
            P("section", "fsdp"),
            P("groups", None),
            P("groups", None),
            P("groups", None),
            P(None, "fsdp"),
            P("groups", "fsdp"),
            P("section"),
        ),
        out_specs=(
            P("section", "groups", "fsdp"),
            P("section", "groups", "fsdp"),
            P("section", "groups", "fsdp"),
            P("section", ("groups", "fsdp")),
        ),
        check_vma=False,
    )
```

time: 239 us -> 108 us (0.45)
  waiting for transfers between devices: 111 us -> 0 us
  Pallas kernels: 0 us -> 89 us
  matrix products: 56.4 us -> 0 us
  other arithmetic: 36.4 us -> 0 us
  between operations: 16.4 us -> 1.29 us
  starting transfers between devices: 7.57 us -> 0 us
  local copies, waits for them, and re-layouts: 10.8 us -> 17.8 us
    pallas_call x0 -> x1, Pallas kernels: none -> 89 us  [local(): pl.pallas_call(functools.partial(kernel, sections, shards), out_shape=(ja...]
    ppermute x2 -> x0, waiting for transfers between devices: 64.4 us -> none  [from_behind(): return lax.ppermute(shard, axis, pairs)]
    dot_general x10 -> x0, matrix products: 56.4 us -> none  [the longest x3 13.2 us: add_block(): jnp.dot(lower, table_block, preferred_element_type=jnp.float32)]
    reduce_sum x4 -> x0, other arithmetic: 31 us -> none  [the longest x3 26.9 us: add_block(): amplitude = jnp.sum(jnp.where(matched, seg_amp[:, :, None], 0.0), axis=1)]
    psum x1 -> x0, waiting for transfers between devices: 23.2 us -> none  [local(): lax.psum(partial_value.astype(jnp.bfloat16), 'section').astype(jnp.float32)]
    reduce_scatter x1 -> x0, waiting for transfers between devices: 23.1 us -> none  [local(): lax.psum_scatter(partial_terms.astype(jnp.bfloat16), 'fsdp', scatter_dime...]
    unnamed x16 -> x9, local copies, waits for them, and re-layouts: 4.21 us -> 17.8 us
    ppermute x2 -> x0, starting transfers between devices: 7.41 us -> none  [from_behind(): return lax.ppermute(shard, axis, pairs)]
  transfers between devices with their start and end apart: 6 -> 0, of which waited for: 4 -> 0; matrix products, arithmetic and copies ran while one was open for 16% -> 0% of each run, Pallas kernels for 0% -> 0%
where the time goes in v2:
time: 108 us
  Pallas kernels  89 us (82%)
  local copies, waits for them, and re-layouts  17.8 us (16%)
  between operations  1.29 us (1%)
    pallas_call x1, Pallas kernels, local(): pl.pallas_call(functools.partial(kernel, sections, shards), out_shape=(ja...  89 us
    unnamed x9, local copies, waits for them, and re-layouts  17.8 us

profile of v2, /device:TPU:0, one launch (start us, length us, event | category | flops | bytes accessed | tf_op | source)
XLA Modules:
  0.0 108.1 jit_solution(968931219054559292)
XLA Ops:
  1.3 1.7 %copy.17.index_ref = s32[512,32]{1,0:T(8,128)} copy(s32[512,32]{0,1:T(8,128)} %param.20) | data formatting | bytes 131072 | tf_op args[7]
  3.0 1.7 %copy.18.amp_ref = f32[512,32]{1,0:T(8,128)} copy(f32[512,32]{0,1:T(8,128)} %param.21) | data formatting | bytes 131072 | tf_op args[8]
  4.6 1.5 %copy.19.field_ref = f32[512,2]{1,0:T(8,128)} copy(f32[512,2]{0,1:T(2,128)} %param.22) | data formatting | bytes 8192 | tf_op args[9]
  6.2 89.0 %shard_map.156 = (bf16[1,512,1024]{2,1,0:T(8,128)(2,1)}, bf16[1,512,1024]{2,1,0:T(8,128)(2,1)}, bf16[1,4096,1024]{2,1,0:T(8,128)(2,1)}, f32[1,1024]{1,0:T(1,128)}) custom-call(bf16[1,512,1024]{2,1,0:T(8,128)(2,1)} %act_hbm.1, bf16[1,512,1024]{2,1,0:T(8,128)(2,1)} %grad_hbm.1, bf16[1,2,512,1024]{3,2,1,0:T(8,128)(2,1)} %stash_ref.1, ...), custom_call_target="tpu_custom_call" | custom-call | flops 12884901888 | bytes 20971520 | tf_op jit(solution)/shard_map/pallas_call | solution.py:344
  95.2 2.3 %copy.25 = bf16[1,512,1024]{2,1,0:T(8,128)(2,1)} copy(bf16[1,512,1024]{2,1,0:T(8,128)(2,1)} %get-tuple-element.8) | data formatting | bytes 2097152
  97.4 2.3 %copy.26 = bf16[1,512,1024]{2,1,0:T(8,128)(2,1)} copy(bf16[1,512,1024]{2,1,0:T(8,128)(2,1)} %get-tuple-element.9) | data formatting | bytes 2097152
  99.7 0.0 copy-start
  99.7 7.8 %copy.27 = bf16[1,4096,1024]{2,1,0:T(8,128)(2,1)} copy(bf16[1,4096,1024]{2,1,0:T(8,128)(2,1)} %get-tuple-element.10) | data formatting | bytes 16777216
  107.5 0.0 copy-done
  107.5 0.6 copy.28
Async XLA Ops:
  99.7 7.8 %copy-start = (f32[1,1024]{1,0:T(1,128)S(1)}, f32[1,1024]{1,0:T(1,128)}, u32[]{:S(2)}) copy-start(f32[1,1024]{1,0:T(1,128)} %get-tuple-element.11) | copy-start | bytes 12292

commit v3 on v2

--- a/solution.py
+++ b/solution.py
@@ -27,11 +27,12 @@
 
 def kernel(
     sections, shards,
-    act_hbm, grad_hbm, stash_ref, pre_ref, weight_hbm, bias_ref, table_ref, index_ref, amp_ref,
-    field_ref, angle_ref, target_ref, sched_ref,
+    act_hbm, grad_hbm, stash_ref, pre_ref, weight_hbm, bias_ref, table_ref, index_in, amp_in,
+    field_in, angle_ref, target_ref, sched_ref,
     fwd_ref, grad_in_ref, grad_w_hbm, grad_bias_ref,
     weight, feat, stash, from_next, matrix, emb, emb_recv, emb_send, pre_grad,
     part_send, part_recv, own, x_recv, grad_w,
+    index_ref, amp_ref, field_ref,
     load_sem, z_send, z_recv, near_send, near_recv, far_send, far_recv, pass_send, pass_recv,
     part_send_sem, part_recv_sem, sum_send_sem, sum_recv_sem, store_sem,
 ):
@@ -131,6 +132,12 @@
     for c in range(CHUNKS):
         stash[me, span(c), :] = jnp.where(slot == 0, stash_ref[0, 0, span(c), :], stash_ref[0, 1, span(c), :])
         gather_start(0, stash, c)
+
+    for c in range(rows // 128):
+        at = pl.ds(c * 128, 128)
+        index_ref[at, :] = index_in[:, at].T
+        amp_ref[at, :] = amp_in[:, at].T
+        field_ref[at, :] = field_in[:, at].T
 
     table_rows = table_ref.shape[0]
     wide = matrix.shape[1]
@@ -331,6 +338,22 @@
             emb_copy(c).wait_send()
 
 
+def copy_kernel(pieces, a, b, c, d, a_out, b_out, c_out, d_out, sem):
+    copies = []
+    for source, target, count in zip((c, a, b), (c_out, a_out, b_out), (pieces[2], pieces[0], pieces[1])):
+        size = source.shape[1] // count
+        for i in range(count):
+            at = pl.ds(i * size, size)
+            copies.append(
+                pltpu.make_async_copy(source.at[0, at], target.at[0, at], sem.at[len(copies)])
+            )
+    copies.append(pltpu.make_async_copy(d, d_out, sem.at[len(copies)]))
+    for copy in copies:
+        copy.start()
+    for copy in copies:
+        copy.wait()
+
+
 def local(sections, shards, *args):
     rows, width = args[0].shape[1:]
     table_rows = args[6].shape[0]
@@ -341,7 +364,9 @@
     smem = pl.BlockSpec(memory_space=pltpu.SMEM)
     dma = pltpu.SemaphoreType.DMA
     half, full = jnp.bfloat16, jnp.float32
-    return pl.pallas_call(
+    args = list(args)
+    inputs = args[:7] + [args[7].T, args[8].T, jnp.pad(args[9].T, ((0, 6), (0, 0)))] + args[10:]
+    results = pl.pallas_call(
         functools.partial(kernel, sections, shards),
         out_shape=(
             jax.ShapeDtypeStruct((1, rows, width), half),
@@ -366,6 +391,9 @@
             pltpu.VMEM((chips, rows, width), half),
             pltpu.VMEM((chips - 1, rows, width), half),
             pltpu.VMEM((shards * width, width), half),
+            pltpu.VMEM((rows, args[7].shape[1]), jnp.int32),
+            pltpu.VMEM((rows, args[7].shape[1]), full),
+            pltpu.VMEM((rows, 8), full),
             dma,
             dma((3, CHUNKS)),
             dma((3, CHUNKS)),
@@ -387,7 +415,16 @@
         cost_estimate=pl.CostEstimate(
             flops=6 * rows * shards * width * width, bytes_accessed=40 * rows * width, transcendentals=0
         ),
-    )(*args)
+    )(*inputs)
+    pieces = (2, 2, 8)
+    return pl.pallas_call(
+        functools.partial(copy_kernel, pieces),
+        out_shape=tuple(jax.ShapeDtypeStruct(r.shape, r.dtype) for r in results),
+        in_specs=[hbm] * 4,
+        out_specs=(hbm,) * 4,
+        scratch_shapes=[dma((sum(pieces) + 1,))],
+        cost_estimate=pl.CostEstimate(flops=0, bytes_accessed=40 * rows * width, transcendentals=0),
+    )(*results)
 
 
 def solution(mesh):

time: 108 us -> 411 us (3.81)
  Pallas kernels: 89 us -> 408 us
  local copies, waits for them, and re-layouts: 17.8 us -> 1.3 us
    pallas_call x0 -> x1, Pallas kernels: none -> 319 us  [local(): pl.pallas_call(functools.partial(copy_kernel, pieces), out_shape=tuple((j...]
    unnamed x9 -> x0, local copies, waits for them, and re-layouts: 17.8 us -> none
where the time goes in v3:
time: 411 us
  Pallas kernels  408 us (99%)
    pallas_call x1, Pallas kernels, local(): pl.pallas_call(functools.partial(copy_kernel, pieces), out_shape=tuple((j...  319 us
    pallas_call x1, Pallas kernels, local(): pl.pallas_call(functools.partial(kernel, sections, shards), out_shape=(ja...  88.9 us

profile of v3, /device:TPU:0, one launch (start us, length us, event | category | flops | bytes accessed | tf_op | source)
XLA Modules:
  0.0 410.6 jit_solution(6810175051565764712)
XLA Ops:
  1.3 1.3 pad.4.field_in
  2.6 88.9 %shard_map.156 = (bf16[1,512,1024]{2,1,0:T(8,128)(2,1)}, bf16[1,512,1024]{2,1,0:T(8,128)(2,1)}, bf16[1,4096,1024]{2,1,0:T(8,128)(2,1)}, f32[1,1024]{1,0:T(1,128)}) custom-call(bf16[1,512,1024]{2,1,0:T(8,128)(2,1)} %act_hbm.1, bf16[1,512,1024]{2,1,0:T(8,128)(2,1)} %grad_hbm.1, bf16[1,2,512,1024]{3,2,1,0:T(8,128)(2,1)} %stash_ref.1, ...), custom_call_target="tpu_custom_call" | custom-call | flops 12884901888 | bytes 20971520 | tf_op jit(solution)/shard_map/pallas_call | solution.py:369
  91.4 319.0 %shard_map.157 = (bf16[1,512,1024]{2,1,0:T(8,128)(2,1)}, bf16[1,512,1024]{2,1,0:T(8,128)(2,1)}, bf16[1,4096,1024]{2,1,0:T(8,128)(2,1)}, f32[1,1024]{1,0:T(1,128)}) custom-call(bf16[1,512,1024]{2,1,0:T(8,128)(2,1)} %get-tuple-element.8.a, bf16[1,512,1024]{2,1,0:T(8,128)(2,1)} %get-tuple-element.9.b, bf16[1,4096,1024]{2,1,0:T(8,128)(2,1)} %get-tuple-element.10.c, ...), custom_call_target="tpu_custom_call" | custom-call | bytes 20971520 | tf_op jit(solution)/shard_map/pallas_call | solution.py:420
